TPU v7x, 512 devices: a whole 4x4x16 slice. The times are simulated.
512 devices in a mesh: frames: 64 (over z, y_hi, core), mp: 4 (over x), dp: 2 (over y_lo).
Axes of the slice: x: 4, y: 4 (y_hi: 2, y_lo: 2; y = y_hi * 2 + y_lo), z: 16, core: 2. Of those that a mesh axis runs over, the one named last changes fastest.
Arguments:
- projections: bfloat16 [2, 128, 96, 3, 3584], P('dp', 'frames', None, None, 'mp'), may hold values from -18 to 18
- perturbation: bfloat16 [2, 128, 96, 3, 3584], P('dp', 'frames', None, None, 'mp'), may hold values from -44 to 44
- out_weight: bfloat16 [3584, 3584], P('frames', 'mp'), may hold values from -0.09375 to 0.09375
- norm_gain: float32 [3584], P('mp'), may hold values from 0.25 to 1.75
- live_counts: int32 [2, 128], P('dp'), may hold values from 72 to 96, as said below
Outputs:
- features: bfloat16 [2, 128, 96, 3584], P('dp', 'frames', None, 'mp')
- penalty: float32 [2], P('dp')
- gain_grad: float32 [3584], P('mp')
Inputs may be any that keep to these rules, and one draw needn't show every extreme that they name: `live_counts`: in each clip one slot has all 96 tokens live and another has 72 live.
All inputs are finite; a program needn't handle non-finite values.
Results may differ from a plain program's by a relative error of at most 0.0057.
Values may be sent and summed in bfloat16 or wider, within the bound.
A program may use at most 64 MiB of HBM per device.

v0:
```python
import math

import jax
import jax.numpy as jnp
from jax import lax
from jax.sharding import PartitionSpec as P

HEAD_DIM = 128


sigma_noise = 0.25
epsilon = 1e-06


def padded(cells, sides, width):
    for axis, dim in sides:
        count = lax.axis_size(axis)
        ends = count - 1
        head = lax.slice_in_dim(cells, 0, width, axis=dim)
        tail = lax.slice_in_dim(cells, cells.shape[dim] - width, cells.shape[dim], axis=dim)
        cells = jnp.concatenate(
            [
                lax.ppermute(tail, axis, [(i, (i + 1) % count) for i in range(ends)]),
                cells,
                lax.ppermute(head, axis, [((i + 1) % count, i) for i in range(ends)]),
            ],
            axis=dim,
        )
    return cells


def split_heads(tensor):
    return tensor.reshape(tensor.shape[:-1] + (tensor.shape[-1] // HEAD_DIM, HEAD_DIM))


def attend(query_rows, key_rows, value_rows, key_live):
    scores = jnp.einsum(
        "wrhe,wmhe->whrm",
        split_heads(query_rows),
        split_heads(key_rows),
        preferred_element_type=jnp.float32,
    ) * (1.0 / math.sqrt(HEAD_DIM))
    live_float = key_live[:, None, None, :]
    masked = jnp.where(live_float, scores, -1e30)
    largest = jnp.max(masked, axis=-1, keepdims=True)
    weights = jnp.exp(masked - largest) * live_float.astype(jnp.float32)
    probabilities = (weights / jnp.sum(weights, axis=-1, keepdims=True)).astype(jnp.bfloat16)
    mixed = jnp.einsum(
        "whrm,wmhe->wrhe",
        probabilities,
        split_heads(value_rows),
        preferred_element_type=jnp.float32,
    )
    return mixed.astype(jnp.bfloat16).reshape(query_rows.shape)


def attend_each(query_rows, key_rows, value_rows, key_live):

    def one_window(item):
        return attend(item[0][None], item[1][None], item[2][None], item[3][None])[0]

    return lax.map(one_window, (query_rows, key_rows, value_rows, key_live))


def local(projections, perturbation, out_weight, norm_gain, live_counts):
    tile_len = projections.shape[2]
    local_width = projections.shape[4]
    slab_count = lax.axis_size("frames")
    slab_index = lax.axis_index("frames")
    model_width = local_width * lax.axis_size("mp")
    token_total = projections.shape[1] * slab_count * tile_len
    perturbed = (
        projections.astype(jnp.float32) + sigma_noise * perturbation.astype(jnp.float32)
    ).astype(jnp.bfloat16)
    streams = jnp.concatenate([projections, perturbed], axis=0)
    padded_counts = jnp.pad(live_counts[0], (1, 1))
    nearby = lax.dynamic_slice_in_dim(padded_counts, 2 * slab_index, 4)
    token_pos = jnp.arange(tile_len)
    live_near = token_pos[None, :] < nearby[:, None]
    key_values = streams[:, :, :, 1:, :]
    widened = padded(key_values, (("frames", 1),), 1)
    grouped = widened.reshape(4, 2 * tile_len, 2, local_width)
    query_rows = streams[:, :, :, 0, :].reshape(4, tile_len, local_width)
    key_live = jnp.tile(live_near.reshape(2, 2 * tile_len), (2, 1))
    attended = attend_each(query_rows, grouped[:, :, 0], grouped[:, :, 1], key_live)
    attended = attended.reshape(2, 2, tile_len, local_width)
    gathered = lax.all_gather(attended, "mp", axis=3, tiled=True)
    flat_rows = gathered.reshape(-1, model_width)
    projected = jnp.dot(
        flat_rows,
        lax.all_gather(out_weight, "frames", axis=0, tiled=True),
        preferred_element_type=jnp.float32,
    )
    projected = projected.reshape(2, 2, tile_len, local_width)
    squares = lax.psum(jnp.sum(projected * projected, axis=-1), "mp")
    normed = projected * lax.rsqrt(squares / model_width + epsilon)[..., None]
    own_live = live_near[1:3].astype(jnp.float32)[:, :, None]
    features = (normed[0] * norm_gain * own_live).astype(jnp.bfloat16)[None]
    difference = (normed[1] - normed[0]) * own_live
    feature_sums = jnp.sum(difference * difference, axis=(0, 1))
    local_penalty = jnp.sum(feature_sums * norm_gain * norm_gain).reshape(1)
    penalty = lax.psum(local_penalty, ("frames", "mp")) / (
        sigma_noise * sigma_noise * token_total * model_width
    )
    gain_grad = (
        norm_gain
        * lax.psum(feature_sums, ("frames", "dp"))
        / (sigma_noise * sigma_noise * token_total)
    )
    return (features, penalty, gain_grad)


def solution(mesh):
    placed = (
        P("dp", "frames", None, None, "mp"),
        P("dp", "frames", None, None, "mp"),
        P("frames", "mp"),
        P("mp"),
        P("dp", None),
    )
    return jax.shard_map(
        local,
        mesh=mesh,
        in_specs=placed,
        out_specs=(P("dp", "frames", None, "mp"), P("dp"), P("mp")),
        check_vma=False,
    )
```

profile of v0, /device:TPU:1, one launch (start us, length us, event | category | flops | bytes accessed | tf_op | source)
XLA Modules:
  0.0 1182.9 jit_solution(10483000948008665854)
XLA Ops:
  7.2 1.9 add_convert_fusion
  9.2 1.2 fusion.25
  10.4 6.2 collective-permute-start
  16.6 4.7 collective-permute-start.1
  22.0 10.1 collective-permute-done
  32.2 1.7 pad_maximum_fusion
  34.1 1.3 slice_bitcast_fusion
  35.4 22.9 %while.10 = (s32[]{:T(128)}, bf16[4,96,896]{2,1,0:T(8,128)(2,1)}, bf16[4,192,896]{2,1,0:T(8,128)(2,1)}, pred[4,192]{1,0:T(4,128)(4,1)S(1)}, bf16[4,96,896]{2,1,0...) while((s32[]{:T(128)}, bf16[4,96,896]{2,1,0:T(8,128)(2,1)}, bf16[4,192,896]{2,1,0:T(8,128)(2,1)}, ...), condition=%wide.region_3.4_spmd, body=%wide.region_0.3_spmd.sunk | while | flops 67049856 | bytes 5857369 | solution.py:62
  35.4 1.0 constant_dynamic-slice_fusion.5
  37.2 1.5 fusion.45
  39.1 1.4 fusion.46
  40.5 0.7 bitcast_dynamic-update-slice_fusion.2
  41.2 1.0 constant_dynamic-slice_fusion.5
  42.9 1.5 fusion.45
  44.8 1.4 fusion.46
  46.9 1.0 constant_dynamic-slice_fusion.5
  48.6 1.5 fusion.45
  50.5 1.4 fusion.46
  51.9 0.7 bitcast_dynamic-update-slice_fusion.2
  52.6 1.0 constant_dynamic-slice_fusion.5
  54.4 1.5 fusion.45
  56.3 1.4 fusion.46
  57.7 0.7 bitcast_dynamic-update-slice_fusion.2
  58.4 0.7 all-gather.5.cloned.1.call-update
  59.2 48.2 %all-gather.3.cloned.1.call-done = bf16[2,2,96,3584]{3,2,1,0:T(8,128)(2,1)} async-done(((bf16[2,2,96,896]{3,2,1,0:T(8,128)(2,1)}), bf16[2,2,96,3584]{3,2,1,0:T(8,128)(2,1)}) %all-gather.3.cloned.1.call-update) | async-done | bytes 2752528 | tf_op jit(solution)/shard_map/all_gather | solution.py:87
  107.5 162.4 %all-gather.5.cloned.1.call-done = bf16[3584,896]{1,0:T(8,128)(2,1)} async-done(((bf16[56,896]{1,0:T(8,128)(2,1)}), bf16[3584,896]{1,0:T(8,128)(2,1)}) %all-gather.5.cloned.1.call-update) | async-done | bytes 6422544 | tf_op jit(solution)/shard_map/all_gather | solution.py:91
  269.9 6.7 multiply_reduce_fusion
  276.6 8.4 psum.21
  285.4 247.0 %psum.23 = f32[896]{0:T(1024)S(1)} all-reduce(f32[896]{0:T(1024)S(1)} %fusion.29), channel_id=1, replica_groups=mesh['frames'=64,'mp'=4,'dp'=2] {'frames','dp'}, use_global_device_ids=true, to_apply=%region_9.10 | all-reduce | flops 896 | bytes 7168 | tf_op jit(solution)/shard_map/psum | solution.py:107
  532.5 0.8 multiply_convert_fusion
  533.3 1.2 multiply_multiply_fusion.1
  534.5 639.8 %psum.22 = f32[1]{0:T(128)} all-reduce(f32[1]{0:T(128)} %bitcast.11), channel_id=1, replica_groups=mesh['frames'=64,'mp'=4,'dp'=2] {'frames','mp'}, use_global_device_ids=true, to_apply=%region_8.9 | all-reduce | flops 1 | bytes 8 | tf_op jit(solution)/shard_map/psum | solution.py:102
  (53 shorter events, 6.5 us)
Async XLA Ops:
  7.2 2.0 copy-start
  7.2 100.3 %all-gather.3.cloned.1.call-start = ((), (), s32[]{:S(2)}) async-start(), calls=%async_computation | async-start | bytes 3440640 | tf_op jit(solution)/shard_map/all_gather | solution.py:87
  9.2 12.2 %copy-start.2 = (s32[1,128]{1,0:T(1,128)S(1)}, s32[1,128]{1,0:T(1,128)}, u32[]{:S(2)}) copy-start(s32[1,128]{1,0:T(1,128)} %param.11) | copy-start | bytes 1540
  10.4 21.8 %collective-permute-start = (bf16[2,1,96,2,896]{4,2,3,1,0:T(8,128)(2,1)}, bf16[2,1,96,2,896]{4,2,3,1,0:T(8,128)(2,1)}, u32[]{:S(2)}, u32[]{:S(2)}) collective-permute-start(bf16[2,1,96,2,896]{4,2,3,1,0:T(8,128)(2,1)} %get-tuple-element.54), channel_id=1, source_target_pairs={{0,8},{8,16},{16,24},{24,32},{32,40},{40,48},{48,56},{56,64},{64,7... | collective-permute-start | bytes 2064392 | tf_op jit(solution)/shard_map/ppermute | solution.py:23
  16.6 15.6 %collective-permute-start.1 = (bf16[2,1,96,2,896]{4,2,3,1,0:T(8,128)(2,1)}, bf16[2,1,96,2,896]{4,2,3,1,0:T(8,128)(2,1)}, u32[]{:S(2)}, u32[]{:S(2)}) collective-permute-start(bf16[2,1,96,2,896]{4,2,3,1,0:T(8,128)(2,1)} %get-tuple-element.55), channel_id=1, source_target_pairs={{8,0},{16,8},{24,16},{32,24},{40,32},{48,40},{56,48},{64,56},{72,6... | collective-permute-start | bytes 2064392 | tf_op jit(solution)/shard_map/ppermute | solution.py:25
  58.4 211.5 %all-gather.5.cloned.1.call-start = ((), (), s32[]{:S(2)}) async-start(), calls=%async_computation.1 | async-start | bytes 6522880 | tf_op jit(solution)/shard_map/all_gather | solution.py:91
  285.0 247.4 %copy-start.1 = (f32[896]{0:T(1024)S(1)}, f32[896]{0:T(1024)}, u32[]{:S(2)}) copy-start(f32[896]{0:T(1024)} %param.10) | copy-start | bytes 10756
Sparse Core Ops, SparseCore 0:
  58.5 48.9 all-gather.2
  110.6 159.1 all-gather.4
where the time goes:
time: 1190 us; the launch traced here: 1180 us
  blocking collectives  895 us (75%)
  waiting for transfers between devices  221 us (19%)
  matrix products  18.3 us (2%)
  between operations  15.9 us (1%)
  local copies, waits for them, and re-layouts  13.2 us (1%)
    psum x1, blocking collectives, local(): lax.psum(local_penalty, ('frames', 'mp'))  640 us
    psum x1, blocking collectives, local(): lax.psum(feature_sums, ('frames', 'dp'))  247 us
    all_gather x1, waiting for transfers between devices, local(): lax.all_gather(out_weight, 'frames', axis=0, tiled=True)  162 us
    all_gather x1, waiting for transfers between devices, local(): gathered = lax.all_gather(attended, 'mp', axis=3, tiled=True)  48.2 us
  transfers between devices with their start and end apart: 4, of which 3 were waited for; matrix products, arithmetic and copies ran while one was open for 0% of the time, Pallas kernels for 0%

commit v1 on v0

v1 whole, which is shorter than its diff:
```python
import functools
import math

import jax
import jax.numpy as jnp
from jax import lax
from jax.experimental import pallas as pl
from jax.experimental.pallas import tpu as pltpu
from jax.sharding import PartitionSpec as P

MESH = pl.DeviceIdType.MESH
HEAD_DIM = 128
SIGMA = 0.25
EPSILON = 1e-06
NEAR, FAR = 0, 1
BF = jnp.bfloat16
F32 = jnp.float32


def kernel(
    frames,
    clean_ref,
    noise_ref,
    weight_ref,
    gain_ref,
    counts_ref,
    features_ref,
    penalty_ref,
    grad_ref,
    streams,
    halo,
    gathered,
    staged,
    weights,
    total,
    squares,
    inverse,
    rows,
    pair,
    plane,
    points,
    line,
    halo_send,
    halo_recv,
    stage_sem,
    cross_sem,
    ring_send,
    ring_recv,
    relay_send,
    relay_recv,
    x_send,
    x_recv,
    row_send,
    row_recv,
    pair_sem,
    plane_send,
    plane_recv,
    point_send,
    point_recv,
    line_send,
    line_recv,
):
    depth = frames // 4
    tile = clean_ref.shape[2]
    width = clean_ref.shape[3]
    heads = width // HEAD_DIM
    f = lax.axis_index("frames")
    m = lax.axis_index("mp")
    lo = lax.axis_index("dp")
    core = f % 2
    hi = (f // 2) % 2
    z = f // 4
    up = 1 - 2 * core

    def at(z_, hi_, core_, m_, lo_):
        return (z_ * 4 + hi_ * 2 + core_, m_, lo_)

    sibling = at(z, hi, 1 - core, m, lo)
    far = ((f + frames + 2 * core - 1) % frames, m, lo)
    cross = at(z, 1 - hi, core, m, 1 - lo)
    onward = at((z + depth + up) % depth, hi, core, m, lo)

    def send(src, dst, send_sem, recv_sem, device):
        return pltpu.make_async_remote_copy(
            src_ref=src,
            dst_ref=dst,
            send_sem=send_sem,
            recv_sem=recv_sem,
            device_id=device,
            device_id_type=MESH,
        )

    y_peers = [at(z, (hi + a) % 2, core, m, (lo + b) % 2) for a, b in ((0, 1), (1, 0), (1, 1))]
    x_peers = [at(z, hi, core, (m + d) % 4, lo) for d in (1, 2, 3)]
    x_sources = [(m + 4 - d) % 4 for d in (1, 2, 3)]
    plane_peers = [at(z, (hi + a) % 2, core, (m + d) % 4, lo) for a in (0, 1) for d in (1, 2, 3)]
    z_peers = [at((z + d) % depth, hi, core, m, lo) for d in range(1, depth)]

    barrier = pltpu.get_barrier_semaphore()
    partners = [sibling, far] + y_peers + plane_peers + z_peers
    for device in partners:
        pl.semaphore_signal(barrier, inc=1, device_id=device, device_id_type=MESH)

    staged[core] = weight_ref[...].astype(F32)
    streams[0] = clean_ref[...]
    pl.semaphore_wait(barrier, len(partners))

    stage_copy = send(staged.at[core], staged.at[core], stage_sem.at[0], stage_sem.at[1], sibling)
    stage_copy.start()

    near_slot = 1 - core
    far_slot = core
    halo_copies = {}

    def send_halo(stream):
        for kind, slot, device in ((NEAR, near_slot, sibling), (FAR, far_slot, far)):
            halo_copies[kind, stream] = send(
                streams.at[stream, slot, pl.ds(1, 2)],
                halo.at[kind, stream],
                halo_send.at[kind, stream],
                halo_recv.at[kind, stream],
                device,
            )
            halo_copies[kind, stream].start()

    send_halo(0)
    for slot in range(2):
        for part in range(3):
            streams[1, slot, part] = (
                clean_ref[slot, part].astype(F32) + SIGMA * noise_ref[slot, part].astype(F32)
            ).astype(BF)
    send_halo(1)

    band = 2 * weight_ref.shape[0]
    group = width // (2 * band)

    def block(zz, side):
        start = pl.multiple_of((zz % group) * (2 * band) + side * band, 16)
        return weights.at[zz // group, pl.ds(start, band)]

    sides = (hi, 1 - hi)
    ring = {}
    relays = {}
    last = depth // 2 - 1

    def start_ring(chunk, step):
        side = sides[chunk] if step < last else (hi + core) % 2
        here = block((z + depth - up * step) % depth, side)
        ring[chunk, step] = send(
            here, here, ring_send.at[chunk, step], ring_recv.at[chunk, step], onward
        )
        ring[chunk, step].start()

    def service(step):
        for chunk in range(2 if step < last else 1):
            ring[chunk, step].wait_recv()
            side = sides[chunk] if step < last else (hi + core) % 2
            here = block((z + 2 * depth - up * (step + 1)) % depth, side)
            if step + 1 < last:
                start_ring(chunk, step + 1)
            relays[chunk, step] = send(
                here, here, relay_send.at[chunk, step], relay_recv.at[chunk, step], sibling
            )
            relays[chunk, step].start()
        if step + 1 == last:
            start_ring(0, last)

    stage_copy.wait()
    own = block(z, hi)
    own[...] = staged[...].reshape(band, width).astype(BF)
    start_ring(0, 0)
    cross_copy = send(own, own, cross_sem.at[0], cross_sem.at[1], cross)
    cross_copy.start()

    def live_count(index):
        inside = (index >= 0) & (index < 2 * frames)
        safe = jnp.clip(index, 0, 2 * frames - 1)
        return jnp.where(inside, counts_ref[0, safe], 0)

    own_slots = (near_slot, far_slot)
    own_counts = (live_count(2 * f + near_slot), live_count(2 * f + far_slot))
    other_counts = (live_count(2 * f + 2 - 3 * core), live_count(2 * f - 1 + 3 * core))
    scale = math.log2(math.e) / math.sqrt(HEAD_DIM)
    nt = (((1,), (1,)), ((), ()))
    nn = (((1,), (0,)), ((), ()))
    key_index = lax.broadcasted_iota(jnp.int32, (tile, tile), 1)

    def attention(kind, stream):
        slot = own_slots[kind]
        halo_copies[kind, stream].wait_recv()
        live_own = key_index < own_counts[kind]
        live_other = key_index < other_counts[kind]
        for h in range(heads):
            lanes = slice(h * HEAD_DIM, (h + 1) * HEAD_DIM)
            query = streams[stream, slot, 0, :, lanes]
            s_own = lax.dot_general(
                query, streams[stream, slot, 1, :, lanes], nt, preferred_element_type=F32
            )
            s_other = lax.dot_general(
                query, halo[kind, stream, 0, :, lanes], nt, preferred_element_type=F32
            )
            s_own = jnp.where(live_own, s_own * scale, -1e30)
            s_other = jnp.where(live_other, s_other * scale, -1e30)
            largest = jnp.max(jnp.maximum(s_own, s_other), axis=1, keepdims=True)
            p_own = jnp.exp2(s_own - largest)
            p_other = jnp.exp2(s_other - largest)
            norm = 1.0 / jnp.sum(p_own + p_other, axis=1, keepdims=True)
            mixed = lax.dot_general(
                (p_own * norm).astype(BF),
                streams[stream, slot, 2, :, lanes],
                nn,
                preferred_element_type=F32,
            ) + lax.dot_general(
                (p_other * norm).astype(BF),
                halo[kind, stream, 1, :, lanes],
                nn,
                preferred_element_type=F32,
            )
            gathered[m, kind, stream, :, lanes] = mixed.astype(BF)

    x_copies = []

    def send_attended(kind):
        for d in range(3):
            copy = send(
                gathered.at[m, kind],
                gathered.at[m, kind],
                x_send.at[kind, d],
                x_recv.at[kind, d],
                x_peers[d],
            )
            copy.start()
            x_copies.append(copy)

    attention(NEAR, 0)
    attention(NEAR, 1)
    send_attended(NEAR)
    cross_copy.wait()
    start_ring(1, 0)
    service(0)
    service(1)
    service(2)
    attention(FAR, 0)
    service(3)
    attention(FAR, 1)
    send_attended(FAR)
    for step in range(4, last + 1):
        service(step)

    for copy in halo_copies.values():
        copy.wait_send()
    for copy in ring.values():
        copy.wait_send()
    for copy in relays.values():
        copy.wait()
    for copy in x_copies:
        copy.wait()

    total[...] = jnp.zeros_like(total)

    @pl.loop(0, 4)
    def _(k):
        total[...] += jnp.dot(
            gathered[k].reshape(4 * tile, width), weights[k], preferred_element_type=F32
        )

    for g in range(4):
        part = jnp.zeros((tile, HEAD_DIM), F32)
        for h in range(heads):
            value = total[g * tile : (g + 1) * tile, h * HEAD_DIM : (h + 1) * HEAD_DIM]
            part += value * value
        squares[g * tile : (g + 1) * tile] = part
    rows[m] = jnp.sum(squares[...].T, axis=0, keepdims=True)
    row_copies = [
        send(rows.at[m], rows.at[m], row_send.at[d], row_recv.at[d], x_peers[d]) for d in range(3)
    ]
    for copy in row_copies:
        copy.start()
    for copy in row_copies:
        copy.wait()
    square = rows[0] + rows[1] + rows[2] + rows[3]
    inverse_row = lax.rsqrt(square / (4 * width) + EPSILON)
    inverse[...] = jnp.broadcast_to(inverse_row, (HEAD_DIM, 4 * tile)).T

    token = lax.broadcasted_iota(jnp.int32, (tile, HEAD_DIM), 0)
    for h in range(heads):
        lanes = slice(h * HEAD_DIM, (h + 1) * HEAD_DIM)
        gain = gain_ref[:, lanes]
        sums = jnp.zeros((1, HEAD_DIM), F32)
        for kind in range(2):
            live = (token < own_counts[kind]).astype(F32)
            base = 2 * kind * tile
            first, second = slice(base, base + tile), slice(base + tile, base + 2 * tile)
            normed = total[first, lanes] * inverse[first]
            features_ref[own_slots[kind], :, lanes] = (normed * gain * live).astype(BF)
            difference = (total[second, lanes] * inverse[second] - normed) * live
            sums += jnp.sum(difference * difference, axis=0, keepdims=True)
        pair[core, :, lanes] = sums

    pair_copy = send(pair.at[core], pair.at[core], pair_sem.at[0], pair_sem.at[1], sibling)
    pair_copy.start()
    pair_copy.wait()
    gain = gain_ref[...]
    pair_sum = pair[0] + pair[1]
    point = jnp.broadcast_to(
        jnp.sum(gain * gain * pair_sum, axis=1, keepdims=True), (1, HEAD_DIM)
    )
    y = hi * 2 + lo
    spot = m * 2 + hi
    plane[y] = jnp.concatenate([pair_sum, point], axis=1)
    points[spot] = point
    copies = [
        send(plane.at[y], plane.at[y], plane_send.at[i], plane_recv.at[i], y_peers[i])
        for i in range(3)
    ] + [
        send(points.at[spot], points.at[spot], point_send.at[i], point_recv.at[i], plane_peers[i])
        for i in range(6)
    ]
    for copy in copies:
        copy.start()
    for copy in copies:
        copy.wait()
    points[m * 2 + 1 - hi] = plane[(1 - hi) * 2 + lo, :, width:]
    point = points[0]
    for i in range(1, 8):
        point = point + points[i]
    plane_sum = plane[0] + plane[1] + plane[2] + plane[3]
    line[z] = jnp.concatenate([plane_sum[:, :width], point], axis=1)
    copies = [
        send(line.at[z], line.at[z], line_send.at[i], line_recv.at[i], z_peers[i])
        for i in range(depth - 1)
    ]
    for copy in copies:
        copy.start()
    for copy in copies:
        copy.wait()
    line_sum = line[0]
    for i in range(1, depth):
        line_sum = line_sum + line[i]
    tokens = 2.0 * frames * tile
    grad_ref[...] = gain * line_sum[:, :width] * (1.0 / (SIGMA * SIGMA * tokens))
    penalty_ref[...] = line_sum[:, width:] * (1.0 / (SIGMA * SIGMA * tokens * 4 * width))


def local(projections, perturbation, out_weight, norm_gain, live_counts):
    frames = lax.axis_size("frames")
    depth = frames // 4
    _, slots, tile, _, width = projections.shape
    clean = jnp.transpose(projections[0], (0, 2, 1, 3))
    noise = jnp.transpose(perturbation[0], (0, 2, 1, 3))
    steps = depth // 2
    dma = pltpu.SemaphoreType.DMA
    vmem = pl.BlockSpec(memory_space=pltpu.VMEM)
    features, penalty, grad = pl.pallas_call(
        functools.partial(kernel, frames),
        out_shape=(
            jax.ShapeDtypeStruct((slots, tile, width), BF),
            jax.ShapeDtypeStruct((1, HEAD_DIM), F32),
            jax.ShapeDtypeStruct((1, width), F32),
        ),
        in_specs=[vmem, vmem, vmem, vmem, pl.BlockSpec(memory_space=pltpu.SMEM)],
        out_specs=(vmem, vmem, vmem),
        scratch_shapes=[
            pltpu.VMEM((2, 2, 3, tile, width), BF),
            pltpu.VMEM((2, 2, 2, tile, width), BF),
            pltpu.VMEM((4, 2, 2, tile, width), BF),
            pltpu.VMEM((2, out_weight.shape[0], width), F32),
            pltpu.VMEM((4, width, width), BF),
            pltpu.VMEM((4 * tile, width), F32),
            pltpu.VMEM((4 * tile, HEAD_DIM), F32),
            pltpu.VMEM((4 * tile, HEAD_DIM), F32),
            pltpu.VMEM((4, 1, 4 * tile), F32),
            pltpu.VMEM((2, 1, width), F32),
            pltpu.VMEM((4, 1, width + HEAD_DIM), F32),
            pltpu.VMEM((8, 1, HEAD_DIM), F32),
            pltpu.VMEM((depth, 1, width + HEAD_DIM), F32),
            dma((2, 2)),
            dma((2, 2)),
            dma((2,)),
            dma((2,)),
            dma((2, steps)),
            dma((2, steps)),
            dma((2, steps)),
            dma((2, steps)),
            dma((2, 3)),
            dma((2, 3)),
            dma((3,)),
            dma((3,)),
            dma((2,)),
            dma((3,)),
            dma((3,)),
            dma((6,)),
            dma((6,)),
            dma((depth - 1,)),
            dma((depth - 1,)),
        ],
        compiler_params=pltpu.CompilerParams(
            collective_id=0, has_side_effects=True, vmem_limit_bytes=48 * 1024 * 1024
        ),
        name="attend_project_reduce",
    )(clean, noise, out_weight, norm_gain.reshape(1, width), live_counts)
    return features[None], penalty[0, :1], grad[0]


def solution(mesh):
    placed = (
        P("dp", "frames", None, None, "mp"),
        P("dp", "frames", None, None, "mp"),
        P("frames", "mp"),
        P("mp"),
        P("dp", None),
    )
    return jax.shard_map(
        local,
        mesh=mesh,
        in_specs=placed,
        out_specs=(P("dp", "frames", None, "mp"), P("dp"), P("mp")),
        check_vma=False,
    )
```

time: 1190 us -> 109 us (0.09)
  blocking collectives: 895 us -> 0 us
  waiting for transfers between devices: 221 us -> 0 us
  Pallas kernels: 0 us -> 101 us
  matrix products: 18.3 us -> 0 us
  between operations: 15.9 us -> 1.82 us
    psum x3 -> x0, blocking collectives: 895 us -> none  [the longest x1 640 us: local(): lax.psum(local_penalty, ('frames', 'mp'))]
    all_gather x2 -> x0, waiting for transfers between devices: 211 us -> none  [the longest x1 162 us: local(): lax.all_gather(out_weight, 'frames', axis=0, tiled=True)]
    pallas_call x0 -> x1, Pallas kernels: none -> 101 us  [local(): pl.pallas_call(functools.partial(kernel, frames), out_shape=(jax.ShapeDty...]
    dot_general x5 -> x0, matrix products: 12.3 us -> none  [the longest x1 6.75 us: local(): jnp.dot(flat_rows, lax.all_gather(out_weight, 'frames', axis=0, tiled=Tru...]
  transfers between devices with their start and end apart: 4 -> 0, of which waited for: 3 -> 0; matrix products, arithmetic and copies ran while one was open for 0% -> 0% of each run, Pallas kernels for 0% -> 0%
where the time goes in v1:
time: 109 us; the launch traced here: 108 us
  Pallas kernels  101 us (93%)
  local copies, waits for them, and re-layouts  4.76 us (4%)
  between operations  1.82 us (2%)
    pallas_call x1, Pallas kernels, local(): pl.pallas_call(functools.partial(kernel, frames), out_shape=(jax.ShapeDty...  101 us
    unnamed x9, local copies, waits for them, and re-layouts  4.06 us

profile of v1, /device:TPU:1, one launch (start us, length us, event | category | flops | bytes accessed | tf_op | source)
XLA Modules:
  0.0 108.4 jit_solution(1117844301753831250)
XLA Ops:
  0.6 0.0 copy-start.3
  0.6 0.7 reshape.9.gain_ref
  1.3 0.0 copy-done.3
  1.3 0.0 copy-start
  1.3 1.2 %copy-done = bf16[1,2,96,3,896]{4,2,3,1,0:T(8,128)(2,1)S(1)} copy-done((bf16[1,2,96,3,896]{4,2,3,1,0:T(8,128)(2,1)S(1)}, bf16[1,2,96,3,896]{4,2,3,1,0:T(8,128)(2,1)}, u32[]{:S(2)}) %copy-start) | copy-done | bytes 1032216
  2.6 0.0 copy-start.1
  2.6 1.2 %copy-done.1 = bf16[1,2,96,3,896]{4,2,3,1,0:T(8,128)(2,1)S(1)} copy-done((bf16[1,2,96,3,896]{4,2,3,1,0:T(8,128)(2,1)S(1)}, bf16[1,2,96,3,896]{4,2,3,1,0:T(8,128)(2,1)}, u32[]{:S(2)}) %copy-start.1) | copy-done | bytes 1032216
  3.8 0.0 copy-start.2
  3.8 0.9 copy-done.2
  4.7 101.2 %attend_project_reduce.1 = (bf16[2,96,896]{2,1,0:T(8,128)(2,1)S(1)}, f32[1,128]{1,0:T(1,128)S(1)}, f32[1,896]{1,0:T(1,128)S(1)}) custom-call(bf16[2,3,96,896]{3,2,1,0:T(8,128)(2,1)S(1)} %bitcast.9, bf16[2,3,96,896]{3,2,1,0:T(8,128)(2,1)S(1)} %bitcast.10, bf16[56,896]{1,0:T(8,128)(2,1)S(1)} %copy-done.2, f32[1,896]{1,0:T(1,128)S(1)} %reshape.9.gain_ref, ...), custom_call_target="tpu_custom_call" | custom-call | tf_op jit(solution)/shard_map/attend_project_reduce/pallas_call | solution.py:354
  105.9 0.6 reduce
  106.5 0.7 copy.10
Async XLA Ops:
  0.6 0.7 copy-start.3
  1.3 1.2 %copy-start = (bf16[1,2,96,3,896]{4,2,3,1,0:T(8,128)(2,1)S(1)}, bf16[1,2,96,3,896]{4,2,3,1,0:T(8,128)(2,1)}, u32[]{:S(2)}) copy-start(bf16[1,2,96,3,896]{4,2,3,1,0:T(8,128)(2,1)} %param.5) | copy-start | bytes 3096580
  2.6 1.2 %copy-start.1 = (bf16[1,2,96,3,896]{4,2,3,1,0:T(8,128)(2,1)S(1)}, bf16[1,2,96,3,896]{4,2,3,1,0:T(8,128)(2,1)}, u32[]{:S(2)}) copy-start(bf16[1,2,96,3,896]{4,2,3,1,0:T(8,128)(2,1)} %param.6) | copy-start | bytes 3096580
  3.8 0.9 copy-start.2

commit v2 on v1

v2 whole, which is shorter than its diff:
```python
import functools
import math

import jax
import jax.numpy as jnp
from jax import lax
from jax.experimental import pallas as pl
from jax.experimental.pallas import tpu as pltpu
from jax.sharding import PartitionSpec as P

MESH = pl.DeviceIdType.MESH
HEAD_DIM = 128
SIGMA = 0.25
EPSILON = 1e-06
NEAR, FAR = 0, 1
BF = jnp.bfloat16
F32 = jnp.float32


def kernel(
    frames,
    clean_ref,
    noise_ref,
    weight_ref,
    gain_ref,
    counts_ref,
    features_ref,
    penalty_ref,
    grad_ref,
    streams,
    noise,
    halo,
    gathered,
    raw,
    weights,
    total,
    squares,
    inverse,
    rows,
    gains,
    counts,
    pair,
    plane,
    points,
    line,
    load_sem,
    halo_send,
    halo_recv,
    raw_send,
    raw_recv,
    ring_send,
    ring_recv,
    relay_send,
    relay_recv,
    x_send,
    x_recv,
    row_send,
    row_recv,
    pair_sem,
    plane_send,
    plane_recv,
    point_send,
    point_recv,
    line_send,
    line_recv,
):
    depth = frames // 4
    tile = clean_ref.shape[2]
    width = clean_ref.shape[3]
    heads = width // HEAD_DIM
    f = lax.axis_index("frames")
    m = lax.axis_index("mp")
    lo = lax.axis_index("dp")
    core = f % 2
    hi = (f // 2) % 2
    z = f // 4
    up = 1 - 2 * core

    def at(z_, hi_, core_, m_, lo_):
        return (z_ * 4 + hi_ * 2 + core_, m_, lo_)

    sibling = at(z, hi, 1 - core, m, lo)
    far = ((f + frames + 2 * core - 1) % frames, m, lo)
    cross = at(z, 1 - hi, core, m, 1 - lo)
    onward = at((z + depth + up) % depth, hi, core, m, lo)

    def send(src, dst, send_sem, recv_sem, device):
        return pltpu.make_async_remote_copy(
            src_ref=src,
            dst_ref=dst,
            send_sem=send_sem,
            recv_sem=recv_sem,
            device_id=device,
            device_id_type=MESH,
        )

    y_peers = [at(z, (hi + a) % 2, core, m, (lo + b) % 2) for a, b in ((0, 1), (1, 0), (1, 1))]
    x_peers = [at(z, hi, core, (m + d) % 4, lo) for d in (1, 2, 3)]
    plane_peers = [at(z, (hi + a) % 2, core, (m + d) % 4, lo) for a in (0, 1) for d in (1, 2, 3)]
    z_peers = [at((z + d) % depth, hi, core, m, lo) for d in range(1, depth)]

    loads = [
        pltpu.make_async_copy(src, dst, load_sem.at[i])
        for i, (src, dst) in enumerate(
            (
                (weight_ref, raw.at[0, core]),
                (clean_ref, streams.at[0]),
                (noise_ref, noise),
                (gain_ref, gains.at[pl.ds(0, heads)]),
                (counts_ref, counts),
            )
        )
    ]
    for load in loads:
        load.start()

    barrier = pltpu.get_barrier_semaphore()
    partners = [sibling, far] + y_peers + plane_peers + z_peers
    for device in partners:
        pl.semaphore_signal(barrier, inc=1, device_id=device, device_id_type=MESH)
    loads[0].wait()
    loads[1].wait()
    pl.semaphore_wait(barrier, len(partners))

    mine = raw.at[0, core]
    theirs = raw.at[1, core]
    raw_copies = [
        send(mine, theirs, raw_send.at[0], raw_recv.at[0], cross),
        send(mine, mine, raw_send.at[1], raw_recv.at[1], sibling),
        send(theirs, theirs, raw_send.at[2], raw_recv.at[2], sibling),
    ]
    raw_copies[0].start()
    raw_copies[1].start()

    near_slot = 1 - core
    far_slot = core
    own_slots = (near_slot, far_slot)
    halo_copies = {}

    def send_halo(kind, stream):
        halo_copies[kind, stream] = send(
            streams.at[stream, own_slots[kind], pl.ds(1, 2)],
            halo.at[kind, stream],
            halo_send.at[kind, stream],
            halo_recv.at[kind, stream],
            (sibling, far)[kind],
        )
        halo_copies[kind, stream].start()

    send_halo(NEAR, 0)
    loads[2].wait()
    for kind in (NEAR, FAR):
        slot = own_slots[kind]
        for part in range(3):
            streams[1, slot, part] = (
                streams[0, slot, part].astype(F32) + SIGMA * noise[slot, part].astype(F32)
            ).astype(BF)
        if kind == NEAR:
            send_halo(NEAR, 1)

    band = 2 * weight_ref.shape[0]
    group = width // (2 * band)
    cuts = ((0, 64), (64, band - 64))

    def block(zz, side, cut):
        start = pl.multiple_of((zz % group) * (2 * band) + side * band + cut[0], 16)
        return weights.at[zz // group, pl.ds(start, cut[1])]

    sides = (hi, 1 - hi)
    last = depth // 2 - 1
    ring = {}
    relays = {}

    def pass_on(side, step, c):
        here = block((z + depth - up * step) % depth, sides[side], cuts[c])
        return send(
            here, here, ring_send.at[side, step, c], ring_recv.at[side, step, c], onward
        )

    def start_ring(side, step):
        for c in range(2):
            ring[side, step, c] = pass_on(side, step, c)
            ring[side, step, c].start()

    def assemble(side):
        joined = jnp.concatenate([raw[side, 0].astype(F32), raw[side, 1].astype(F32)], axis=0)
        block(z, sides[side], (0, band))[...] = joined.astype(BF)
        start_ring(side, 0)

    def final_copies(side):
        return [pass_on(side, last, c) for c in range(2)]

    def relay(side, step):
        for c in range(2):
            here = block((z + 2 * depth - up * (step + 1)) % depth, sides[side], cuts[c])
            yield c, send(
                here, here, relay_send.at[side, step, c], relay_recv.at[side, step, c], sibling
            )

    def service(side, step):
        copies = dict(relay(side, step))
        for c in range(2):
            ring[side, step, c].wait_recv()
            if step + 1 < last:
                ring[side, step + 1, c] = pass_on(side, step + 1, c)
                ring[side, step + 1, c].start()
            else:
                @pl.when(core == side)
                def _():
                    pass_on(side, last, c).start()

            relays[side, step, c] = copies[c]
            relays[side, step, c].start()

    def service_last(side):
        @pl.when(core == side)
        def _():
            copies = dict(relay(side, last))
            for c in range(2):
                pass_on(side, last, c).wait_recv()
                copies[c].start()

    def live_count(index):
        inside = (index >= 0) & (index < 2 * frames)
        safe = jnp.clip(index, 0, 2 * frames - 1)
        return jnp.where(inside, counts[0, safe], 0)

    loads[3].wait()
    loads[4].wait()
    own_counts = (live_count(2 * f + near_slot), live_count(2 * f + far_slot))
    other_counts = (live_count(2 * f + 2 - 3 * core), live_count(2 * f - 1 + 3 * core))
    scale = math.log2(math.e) / math.sqrt(HEAD_DIM)
    nt = (((1,), (1,)), ((), ()))
    nn = (((1,), (0,)), ((), ()))
    key_index = lax.broadcasted_iota(jnp.int32, (tile, tile), 1)
    x_copies = []

    def attention(kind, stream):
        slot = own_slots[kind]
        halo_copies[kind, stream].wait_recv()
        live_own = key_index < own_counts[kind]
        live_other = key_index < other_counts[kind]
        for h in range(heads):
            lanes = slice(h * HEAD_DIM, (h + 1) * HEAD_DIM)
            query = streams[stream, slot, 0, :, lanes]
            s_own = lax.dot_general(
                query, streams[stream, slot, 1, :, lanes], nt, preferred_element_type=F32
            )
            s_other = lax.dot_general(
                query, halo[kind, stream, 0, :, lanes], nt, preferred_element_type=F32
            )
            s_own = jnp.where(live_own, s_own * scale, -1e30)
            s_other = jnp.where(live_other, s_other * scale, -1e30)
            largest = jnp.max(jnp.maximum(s_own, s_other), axis=1, keepdims=True)
            p_own = jnp.exp2(s_own - largest)
            p_other = jnp.exp2(s_other - largest)
            norm = 1.0 / jnp.sum(p_own + p_other, axis=1, keepdims=True)
            mixed = lax.dot_general(
                (p_own * norm).astype(BF),
                streams[stream, slot, 2, :, lanes],
                nn,
                preferred_element_type=F32,
            ) + lax.dot_general(
                (p_other * norm).astype(BF),
                halo[kind, stream, 1, :, lanes],
                nn,
                preferred_element_type=F32,
            )
            gathered[m, kind, stream, :, lanes] = mixed.astype(BF)
        piece = gathered.at[m, kind, stream]
        for d in (1, 0, 2):
            copy = send(
                piece, piece, x_send.at[kind, stream, d], x_recv.at[kind, stream, d], x_peers[d]
            )
            copy.start()
            x_copies.append(copy)

    def wait_relays(side, step):
        for c in range(2):
            relays[side, step, c].wait()

    def multiply(part):
        k = part % 4
        total[...] += jnp.dot(
            gathered[k].reshape(4 * tile, width), weights[k], preferred_element_type=F32
        )

    raw_copies[1].wait()
    assemble(0)
    attention(NEAR, 0)
    raw_copies[0].wait_recv()
    raw_copies[2].start()
    raw_copies[2].wait()
    assemble(1)
    send_halo(FAR, 0)
    send_halo(FAR, 1)
    attention(NEAR, 1)
    service(0, 0)
    service(1, 0)
    service(0, 1)
    service(1, 1)
    service(0, 2)
    attention(FAR, 0)
    service(1, 2)
    service(0, 3)
    service(1, 3)
    service(0, 4)
    attention(FAR, 1)
    total[...] = jnp.zeros_like(total)
    service(1, 4)
    service(0, 5)
    service(1, 5)
    service(0, 6)
    for copy in x_copies:
        copy.wait()
    for step in range(5):
        for side in range(2):
            wait_relays(side, step)
    own_part = z // group
    nearer = jnp.where(z % group >= group // 2, 1, 3)
    multiply(own_part)
    multiply(own_part + nearer)
    service_last(0)
    service(1, 6)
    for step in range(5, last):
        for side in range(2):
            wait_relays(side, step)
    multiply(own_part + 4 - nearer)
    service_last(1)

    gains[heads:] = jnp.zeros((8 - heads, HEAD_DIM), F32)
    raw_copies[0].wait_send()
    for copy in halo_copies.values():
        copy.wait_send()
    for copy in ring.values():
        copy.wait_send()
    for side in range(2):
        copies = dict(relay(side, last))

        @pl.when(core == side)
        def _():
            for c in range(2):
                pass_on(side, last, c).wait_send()
                copies[c].wait_send()

        @pl.when(core != side)
        def _():
            for c in range(2):
                copies[c].wait_recv()

    multiply(own_part + 2)

    for g in range(4):
        part = jnp.zeros((tile, HEAD_DIM), F32)
        for h in range(heads):
            value = total[g * tile : (g + 1) * tile, h * HEAD_DIM : (h + 1) * HEAD_DIM]
            part += value * value
        squares[g * tile : (g + 1) * tile] = part
    rows[m] = jnp.sum(squares[...].T, axis=0, keepdims=True)
    row_copies = [
        send(rows.at[m], rows.at[m], row_send.at[d], row_recv.at[d], x_peers[d]) for d in (1, 0, 2)
    ]
    for copy in row_copies:
        copy.start()
    for copy in row_copies:
        copy.wait()
    square = rows[0] + rows[1] + rows[2] + rows[3]
    inverse_row = lax.rsqrt(square / (4 * width) + EPSILON)
    inverse[...] = jnp.broadcast_to(inverse_row, (HEAD_DIM, 4 * tile)).T

    token = lax.broadcasted_iota(jnp.int32, (tile, HEAD_DIM), 0)
    for h in range(heads):
        lanes = slice(h * HEAD_DIM, (h + 1) * HEAD_DIM)
        sums = jnp.zeros((1, HEAD_DIM), F32)
        for kind in range(2):
            live = (token < own_counts[kind]).astype(F32)
            base = 2 * kind * tile
            first, second = slice(base, base + tile), slice(base + tile, base + 2 * tile)
            normed = total[first, lanes] * inverse[first]
            features_ref[own_slots[kind], :, lanes] = (normed * gains[h : h + 1] * live).astype(BF)
            difference = (total[second, lanes] * inverse[second] - normed) * live
            sums += jnp.sum(difference * difference, axis=0, keepdims=True)
        pair[core, h : h + 1] = sums
    pair[core, heads:] = jnp.zeros((8 - heads, HEAD_DIM), F32)

    pair_copy = send(pair.at[core], pair.at[core], pair_sem.at[0], pair_sem.at[1], sibling)
    pair_copy.start()
    pair_copy.wait()
    gain = gains[...]
    is_sum = lax.broadcasted_iota(jnp.int32, (8, HEAD_DIM), 0) < heads
    pair_sum = pair[0] + pair[1]
    point = jnp.sum(
        jnp.sum(gain * gain * pair_sum, axis=0, keepdims=True), axis=1, keepdims=True
    )
    point = jnp.broadcast_to(point, (1, HEAD_DIM))
    y = hi * 2 + lo
    spot = m * 2 + hi
    plane[y] = jnp.where(is_sum, pair_sum, point)
    points[spot] = point
    copies = [
        send(plane.at[y], plane.at[y], plane_send.at[i], plane_recv.at[i], y_peers[i])
        for i in range(3)
    ] + [
        send(points.at[spot], points.at[spot], point_send.at[i], point_recv.at[i], plane_peers[i])
        for i in range(6)
    ]
    for copy in copies:
        copy.start()
    for copy in copies:
        copy.wait()
    points[m * 2 + 1 - hi] = plane[(1 - hi) * 2 + lo, heads : heads + 1]
    point = points[0]
    for i in range(1, 8):
        point = point + points[i]
    line[z] = jnp.where(is_sum, plane[0] + plane[1] + plane[2] + plane[3], point)
    copies = [
        send(line.at[z], line.at[z], line_send.at[i], line_recv.at[i], z_peers[i])
        for i in sorted(range(depth - 1), key=lambda i: -min(i + 1, depth - 1 - i))
    ]
    for copy in copies:
        copy.start()
    for copy in copies:
        copy.wait()
    line_sum = line[0]
    for i in range(1, depth):
        line_sum = line_sum + line[i]
    tokens = 2.0 * frames * tile
    grad_ref[...] = (gain * line_sum * (1.0 / (SIGMA * SIGMA * tokens)))[:heads]
    penalty_ref[...] = line_sum[heads:] * (1.0 / (SIGMA * SIGMA * tokens * 4 * width))


def local(projections, perturbation, out_weight, norm_gain, live_counts):
    frames = lax.axis_size("frames")
    depth = frames // 4
    _, slots, tile, _, width = projections.shape
    heads = width // HEAD_DIM
    clean = jnp.transpose(projections[0], (0, 2, 1, 3))
    noise = jnp.transpose(perturbation[0], (0, 2, 1, 3))
    steps = depth // 2
    dma = pltpu.SemaphoreType.DMA
    vmem = pl.BlockSpec(memory_space=pltpu.VMEM)
    hbm = pl.BlockSpec(memory_space=pltpu.HBM)
    features, penalty, grad = pl.pallas_call(
        functools.partial(kernel, frames),
        out_shape=(
            jax.ShapeDtypeStruct((slots, tile, width), BF),
            jax.ShapeDtypeStruct((8 - heads, HEAD_DIM), F32),
            jax.ShapeDtypeStruct((heads, HEAD_DIM), F32),
        ),
        in_specs=[hbm, hbm, hbm, hbm, hbm],
        out_specs=(vmem, vmem, vmem),
        scratch_shapes=[
            pltpu.VMEM((2, slots, 3, tile, width), BF),
            pltpu.VMEM((slots, 3, tile, width), BF),
            pltpu.VMEM((2, 2, 2, tile, width), BF),
            pltpu.VMEM((4, 2, 2, tile, width), BF),
            pltpu.VMEM((2, 2, out_weight.shape[0], width), BF),
            pltpu.VMEM((4, width, width), BF),
            pltpu.VMEM((4 * tile, width), F32),
            pltpu.VMEM((4 * tile, HEAD_DIM), F32),
            pltpu.VMEM((4 * tile, HEAD_DIM), F32),
            pltpu.VMEM((4, 1, 4 * tile), F32),
            pltpu.VMEM((8, HEAD_DIM), F32),
            pltpu.SMEM(live_counts.shape, jnp.int32),
            pltpu.VMEM((2, 8, HEAD_DIM), F32),
            pltpu.VMEM((4, 8, HEAD_DIM), F32),
            pltpu.VMEM((8, 1, HEAD_DIM), F32),
            pltpu.VMEM((depth, 8, HEAD_DIM), F32),
            dma((5,)),
            dma((2, 2)),
            dma((2, 2)),
            dma((3,)),
            dma((3,)),
            dma((2, steps, 2)),
            dma((2, steps, 2)),
            dma((2, steps, 2)),
            dma((2, steps, 2)),
            dma((2, 2, 3)),
            dma((2, 2, 3)),
            dma((3,)),
            dma((3,)),
            dma((2,)),
            dma((3,)),
            dma((3,)),
            dma((6,)),
            dma((6,)),
            dma((depth - 1,)),
            dma((depth - 1,)),
        ],
        compiler_params=pltpu.CompilerParams(
            collective_id=0, has_side_effects=True, vmem_limit_bytes=54000 * 1024
        ),
        name="attend_project_reduce",
    )(clean, noise, out_weight, norm_gain.reshape(heads, HEAD_DIM), live_counts)
    return features[None], penalty[0, :1], grad.reshape(width)


def solution(mesh):
    placed = (
        P("dp", "frames", None, None, "mp"),
        P("dp", "frames", None, None, "mp"),
        P("frames", "mp"),
        P("mp"),
        P("dp", None),
    )
    return jax.shard_map(
        local,
        mesh=mesh,
        in_specs=placed,
        out_specs=(P("dp", "frames", None, "mp"), P("dp"), P("mp")),
        check_vma=False,
    )
```

time: 109 us -> 90.3 us (0.83)
  Pallas kernels: 101 us -> 85.4 us
  local copies, waits for them, and re-layouts: 4.76 us -> 2.9 us
    pallas_call x1, Pallas kernels: 101 us -> 85.4 us  [local(): pl.pallas_call(functools.partial(kernel, frames), out_shape=(jax.ShapeDty...]
    unnamed x9 -> x8, local copies, waits for them, and re-layouts: 4.06 us -> 2.9 us
where the time goes in v2:
time: 90.3 us; the launch traced here: 90.1 us
  Pallas kernels  85.4 us (95%)
  local copies, waits for them, and re-layouts  2.9 us (3%)
  between operations  1.83 us (2%)
    pallas_call x1, Pallas kernels, local(): pl.pallas_call(functools.partial(kernel, frames), out_shape=(jax.ShapeDty...  85.4 us
    unnamed x8, local copies, waits for them, and re-layouts  2.9 us

profile of v2, /device:TPU:1, one launch (start us, length us, event | category | flops | bytes accessed | tf_op | source)
XLA Modules:
  0.0 90.1 jit_solution(7270453614839836373)
XLA Ops:
  0.6 0.0 copy-start.1
  0.6 0.0 copy-start.2
  0.7 0.7 copy-done.1
  1.3 0.0 copy-done.2
  1.3 0.0 copy-start
  1.3 0.9 copy-done
  2.2 85.4 %attend_project_reduce.1 = (bf16[2,96,896]{2,1,0:T(8,128)(2,1)S(1)}, f32[1,128]{1,0:T(1,128)S(1)}, f32[7,128]{1,0:T(8,128)S(1)}) custom-call(bf16[2,3,96,896]{3,2,1,0:T(8,128)(2,1)} %bitcast.15, bf16[2,3,96,896]{3,2,1,0:T(8,128)(2,1)} %bitcast.16, bf16[56,896]{1,0:T(8,128)(2,1)S(1)} %copy-done, f32[7,128]{1,0:T(8,128)S(1)} %bitcast.12, s32[1,128]{1,0:T(1,128)S(1)} %copy-done.2), custom_call_target="tpu_custom_call" | custom-call | tf_op jit(solution)/shard_map/attend_project_reduce/pallas_call | solution.py:443
  87.6 0.7 copy.11
  88.4 0.6 copy.13
Async XLA Ops:
  0.6 0.7 copy-start.1
  0.6 0.7 copy-start.2
  1.3 0.9 copy-start

commit v3 on v2

--- a/solution.py
+++ b/solution.py
@@ -204,11 +204,13 @@
             if step + 1 < last:
                 ring[side, step + 1, c] = pass_on(side, step + 1, c)
                 ring[side, step + 1, c].start()
-            else:
+            if step + 1 == last:
+
                 @pl.when(core == side)
                 def _():
                     pass_on(side, last, c).start()
 
+        for c in range(2):
             relays[side, step, c] = copies[c]
             relays[side, step, c].start()
 
@@ -311,6 +313,7 @@
     service(0, 5)
     service(1, 5)
     service(0, 6)
+    service_last(0)
     for copy in x_copies:
         copy.wait()
     for step in range(5):
@@ -319,14 +322,13 @@
     own_part = z // group
     nearer = jnp.where(z % group >= group // 2, 1, 3)
     multiply(own_part)
+    service(1, 6)
+    service_last(1)
     multiply(own_part + nearer)
-    service_last(0)
-    service(1, 6)
     for step in range(5, last):
         for side in range(2):
             wait_relays(side, step)
     multiply(own_part + 4 - nearer)
-    service_last(1)
 
     gains[heads:] = jnp.zeros((8 - heads, HEAD_DIM), F32)
     raw_copies[0].wait_send()
@@ -443,9 +445,9 @@
     features, penalty, grad = pl.pallas_call(
         functools.partial(kernel, frames),
         out_shape=(
-            jax.ShapeDtypeStruct((slots, tile, width), BF),
-            jax.ShapeDtypeStruct((8 - heads, HEAD_DIM), F32),
-            jax.ShapeDtypeStruct((heads, HEAD_DIM), F32),
+            pltpu.VMEM((slots, tile, width), BF),
+            pltpu.VMEM((8 - heads, HEAD_DIM), F32),
+            pltpu.VMEM((heads, HEAD_DIM), F32),
         ),
         in_specs=[hbm, hbm, hbm, hbm, hbm],
         out_specs=(vmem, vmem, vmem),
@@ -488,7 +490,7 @@
             dma((depth - 1,)),
         ],
         compiler_params=pltpu.CompilerParams(
-            collective_id=0, has_side_effects=True, vmem_limit_bytes=54000 * 1024
+            collective_id=0, has_side_effects=True, vmem_limit_bytes=56000 * 1024
         ),
         name="attend_project_reduce",
     )(clean, noise, out_weight, norm_gain.reshape(heads, HEAD_DIM), live_counts)

time: 90.3 us -> 88.3 us (0.978)
  local copies, waits for them, and re-layouts: 2.9 us -> 1.33 us
    unnamed x8 -> x2, local copies, waits for them, and re-layouts: 2.9 us -> 1.33 us
where the time goes in v3:
time: 88.3 us; the launch traced here: 88.2 us
  Pallas kernels  85 us (96%)
  between operations  1.81 us (2%)
  local copies, waits for them, and re-layouts  1.33 us (2%)
    pallas_call x1, Pallas kernels, local(): pl.pallas_call(functools.partial(kernel, frames), out_shape=(pltpu.VMEM((...  85 us

profile of v3, /device:TPU:1, one launch (start us, length us, event | category | flops | bytes accessed | tf_op | source)
XLA Modules:
  0.0 88.2 jit_solution(13393122572987288701)
XLA Ops:
  0.6 85.0 %attend_project_reduce.1 = (bf16[2,96,896]{2,1,0:T(8,128)(2,1)S(1)}, f32[1,128]{1,0:T(1,128)S(1)}, f32[7,128]{1,0:T(8,128)S(1)}) custom-call(bf16[2,3,96,896]{3,2,1,0:T(8,128)(2,1)} %bitcast.14, bf16[2,3,96,896]{3,2,1,0:T(8,128)(2,1)} %bitcast.15, bf16[56,896]{1,0:T(8,128)(2,1)} %weight_ref.1, f32[7,128]{1,0:T(8,128)} %bitcast.16, s32[1,128]{1,0:T(1,128)} %counts_ref.1), custom_call_target="tpu_custom_call" | custom-call | tf_op jit(solution)/shard_map/attend_project_reduce/pallas_call | solution.py:445
  85.7 0.7 copy.11
  86.4 0.6 copy.12

commit v4 on v3

--- a/solution.py
+++ b/solution.py
@@ -292,11 +292,11 @@
     attention(NEAR, 0)
     raw_copies[0].wait_recv()
     raw_copies[2].start()
-    raw_copies[2].wait()
-    assemble(1)
     send_halo(FAR, 0)
     send_halo(FAR, 1)
     attention(NEAR, 1)
+    raw_copies[2].wait()
+    assemble(1)
     service(0, 0)
     service(1, 0)
     service(0, 1)

time: 88.3 us -> 87.4 us (0.990)
  Pallas kernels: 85 us -> 84.1 us
    pallas_call x1, Pallas kernels: 85 us -> 84.1 us  [local(): pl.pallas_call(functools.partial(kernel, frames), out_shape=(pltpu.VMEM((...]
where the time goes in v4:
time: 87.4 us; the launch traced here: 87.2 us
  Pallas kernels  84.1 us (96%)
  between operations  1.81 us (2%)
  local copies, waits for them, and re-layouts  1.33 us (2%)
    pallas_call x1, Pallas kernels, local(): pl.pallas_call(functools.partial(kernel, frames), out_shape=(pltpu.VMEM((...  84.1 us

profile of v4, /device:TPU:1, one launch (start us, length us, event | category | flops | bytes accessed | tf_op | source)
XLA Modules:
  0.0 87.2 jit_solution(9580844347168455069)
XLA Ops:
  0.6 84.1 %attend_project_reduce.1 = (bf16[2,96,896]{2,1,0:T(8,128)(2,1)S(1)}, f32[1,128]{1,0:T(1,128)S(1)}, f32[7,128]{1,0:T(8,128)S(1)}) custom-call(bf16[2,3,96,896]{3,2,1,0:T(8,128)(2,1)} %bitcast.14, bf16[2,3,96,896]{3,2,1,0:T(8,128)(2,1)} %bitcast.15, bf16[56,896]{1,0:T(8,128)(2,1)} %weight_ref.1, f32[7,128]{1,0:T(8,128)} %bitcast.16, s32[1,128]{1,0:T(1,128)} %counts_ref.1), custom_call_target="tpu_custom_call" | custom-call | tf_op jit(solution)/shard_map/attend_project_reduce/pallas_call | solution.py:445
  84.7 0.7 copy.11
  85.5 0.6 copy.12
